TPU v7x, 256 devices: a whole 4x4x8 slice. The times are simulated.
256 devices in a mesh: batch: 32 (over x_hi, z, core), head: 8 (over y, x_lo).
Axes of the slice: x: 4 (x_hi: 2, x_lo: 2; x = x_hi * 2 + x_lo), y: 4, z: 8, core: 2. Of those that a mesh axis runs over, the one named last changes fastest.
Arguments:
- ssm_values: bfloat16 [64, 256, 16384], P('batch', None, 'head'), may hold values from -6 to 6
- ssm_gate: bfloat16 [64, 256, 16384], P('batch', None, 'head'), may hold values from -6 to 6
- ssm_keys: bfloat16 [64, 256, 2048], P('batch', None, 'head'), may hold values from -6 to 6
- ssm_queries: bfloat16 [64, 256, 2048], P('batch', None, 'head'), may hold values from -0.375 to 0.375
- step_sizes: float32 [64, 256, 256], P('batch', None, 'head'), as said below
- decay_rates: float32 [256], P('head'), as said below
- skip_weights: float32 [256], P('head'), may hold values from 0.25 to 1.75
- norm_gain: float32 [16384], P('head'), may hold values from 0.5 to 1.5
- att_queries: bfloat16 [64, 256, 8192], P('batch', None, 'head'), may hold values from -64 to 64
- new_keyvals: bfloat16 [64, 256, 2048], P('batch', None, 'head'), may hold values from -32 to 32
- page_pool: bfloat16 [1024, 1024, 256], P('batch', 'head'), may hold values from -6 to 6
- page_owner: int32 [64, 32, 1], P('batch'), may hold values from 0 to 31; in each aligned block of 64 rows (0 to 63, 64 to 127, ..., all dimensions but the last counted through in order) at most 4 rows name the same one
- page_slot: int32 [64, 32], P('batch'), may hold values from 0 to 31
- new_lengths: int32 [64], P('batch'), may hold values from 64 to 256, as said below
- cached_lengths: int32 [64], P('batch'), may hold values from 128 to 2048, as said below
Outputs:
- mixer_out: bfloat16 [64, 256, 16384], P('batch', None, 'head')
- attention_out: bfloat16 [64, 256, 8192], P('batch', None, 'head')
Inputs may be any that keep to these rules, and one draw needn't show every extreme that they name: `page_owner`: within the rows of one device's requests, no owner is named more than 4 times; in some device's rows one owner is named exactly 4 times. `new_lengths`: some request has 256 new tokens. `cached_lengths`: some request has 2048 cached tokens. `step_sizes`: Positive. `decay_rates`: Positive.
All inputs are finite; a program needn't handle non-finite values.
Results may differ from a plain program's by a relative error of at most 0.0049.
Values may be sent and summed in bfloat16 or wider, within the bound.
No kernel may reach another device: no remote copies, remote signals or barrier semaphores. Data moves between devices by JAX's collectives and lax.ppermute only.
A program may use at most 128 MiB of HBM per device.

v0:
```python
import jax
import jax.numpy as jnp
from jax import lax
from jax.sharding import PartitionSpec as P

HEAD_P = 64
STATE = 256
HEAD_DIM = 128
PAGE = 128
STATE_PAGES = 16
CAP = 4


def mamba_block(
    values,
    gate_rows,
    key_rows,
    query_rows,
    step_rows,
    rate_rows,
    skip_rows,
    gain_rows,
    cached_state,
    length,
):
    new_count = values.shape[0]
    head_count = rate_rows.shape[0]
    group_count = key_rows.shape[1] // STATE
    per_group = head_count // group_count
    decay_sum = jnp.cumsum(step_rows * rate_rows[None, :], axis=0)
    keys_group = key_rows.reshape(new_count, group_count, STATE)
    queries_group = query_rows.reshape(new_count, group_count, STATE)
    inner_prod = jnp.einsum(
        "tgn,sgn->gts", queries_group, keys_group, preferred_element_type=jnp.float32
    )
    inner_prod = jnp.repeat(inner_prod, per_group, axis=0)
    positions = jnp.arange(new_count, dtype=jnp.int32)
    causal = positions[:, None] >= positions[None, :]
    lagged = decay_sum.T
    spread = jnp.where(causal[None], lagged[:, None, :] - lagged[:, :, None], 0.0)
    weights = jnp.where(causal[None], jnp.exp(spread), 0.0) * inner_prod * step_rows.T[:, None, :]
    weights = weights.astype(jnp.bfloat16)
    per_head = values.reshape(new_count, head_count, HEAD_P)
    fresh_part = jnp.einsum("hts,shp->thp", weights, per_head, preferred_element_type=jnp.float32)
    grouped_state = cached_state.reshape(group_count, per_group, HEAD_P, STATE)
    carried = jnp.einsum(
        "tgn,gkpn->tgkp", queries_group, grouped_state, preferred_element_type=jnp.float32
    )
    carried = carried.reshape(new_count, head_count, HEAD_P) * jnp.exp(-decay_sum)[:, :, None]
    mixed_rows = carried + fresh_part + skip_rows[None, :, None] * per_head.astype(jnp.float32)
    gated_rows = mixed_rows * jax.nn.silu(
        gate_rows.reshape(new_count, head_count, HEAD_P).astype(jnp.float32)
    )
    gated_rows = gated_rows.reshape(new_count, group_count, per_group * HEAD_P)
    mean_square = jnp.mean(gated_rows * gated_rows, axis=-1, keepdims=True)
    normed = (
        gated_rows
        * lax.rsqrt(mean_square + 1e-05)
        * gain_rows.reshape(group_count, per_group * HEAD_P)
    )
    normed = jnp.where(positions[:, None, None] < length, normed, 0.0)
    return normed.astype(jnp.bfloat16).reshape(new_count, head_count * HEAD_P)


def attend(queries, fresh_kv, previous_rows, length, cached):
    new_count = queries.shape[0]
    kv_count = fresh_kv.shape[1] // (2 * HEAD_DIM)
    q_group = queries.shape[1] // (HEAD_DIM * kv_count)
    old_count = previous_rows.shape[1]
    new_rows = fresh_kv.reshape(new_count, kv_count, 2 * HEAD_DIM).transpose(1, 0, 2)
    keyvals = jnp.concatenate([previous_rows, new_rows], axis=1)
    grouped_heads = queries.reshape(new_count, kv_count, q_group, HEAD_DIM)
    scores = jnp.einsum(
        "tkgd,ksd->kgts",
        grouped_heads,
        keyvals[:, :, :HEAD_DIM],
        preferred_element_type=jnp.float32,
    ) * HEAD_DIM ** (-0.5)
    positions = jnp.arange(new_count, dtype=jnp.int32)
    old_seen = jnp.broadcast_to(
        jnp.arange(old_count, dtype=jnp.int32)[None, :] < cached, (new_count, old_count)
    )
    new_seen = positions[None, :] <= positions[:, None]
    visible = jnp.concatenate([old_seen, new_seen], axis=1)
    scores = jnp.where(visible, scores, -jnp.inf)
    row_max = jnp.max(scores, axis=-1, keepdims=True)
    raised = jnp.exp(scores - row_max)
    probabilities = (raised / jnp.sum(raised, axis=-1, keepdims=True)).astype(jnp.bfloat16)
    output = jnp.einsum(
        "kgts,ksd->tkgd",
        probabilities,
        keyvals[:, :, HEAD_DIM:],
        preferred_element_type=jnp.float32,
    )
    output = jnp.where(positions[:, None, None, None] < length, output, 0.0)
    return output.astype(jnp.bfloat16).reshape(new_count, kv_count * q_group * HEAD_DIM)


def body(
    ssm_values,
    ssm_gate,
    ssm_keys,
    ssm_queries,
    step_sizes,
    decay_rates,
    skip_weights,
    norm_gain,
    att_queries,
    new_keyvals,
    page_pool,
    page_owner,
    page_slot,
    new_lengths,
    cached_lengths,
):
    owner_count = lax.axis_size("batch")
    my_index = lax.axis_index("batch")
    req_count = ssm_values.shape[0]
    table_width = page_owner.shape[1]
    block_rows = req_count * table_width
    owners = page_owner.reshape(block_rows)
    row_order = jnp.arange(block_rows, dtype=jnp.int32)
    earlier = (owners[:, None] == owners[None, :]) & (row_order[None, :] < row_order[:, None])
    rank_in = jnp.sum(earlier.astype(jnp.int32), axis=1)
    capacity = jnp.arange(CAP, dtype=jnp.int32)
    all_owners, all_slots = (
        lax.all_gather(page_owner, "batch", axis=0, tiled=True),
        lax.all_gather(page_slot, "batch", axis=0, tiled=True),
    )
    owned_rows = (all_owners.reshape(owner_count, block_rows) == my_index).astype(jnp.int32)
    ahead_count = jnp.cumsum(owned_rows, axis=1) - owned_rows
    picked = (owned_rows[:, :, None] == 1) & (ahead_count[:, :, None] == capacity[None, None, :])
    chosen = (
        jnp.sum(
            jnp.where(picked, all_slots.reshape(owner_count, block_rows)[:, :, None] + 1, 0), axis=1
        )
        - 1
    )
    leaving_rows = page_pool[jnp.maximum(chosen, 0)]
    leaving_rows = jnp.where(
        (chosen >= 0)[:, :, None, None], leaving_rows, jnp.zeros((), page_pool.dtype)
    )
    local_rows = leaving_rows.shape[2]
    kv_local = local_rows // PAGE
    arrived = lax.all_to_all(leaving_rows, "batch", split_axis=0, concat_axis=0, tiled=True)
    flattened = arrived.reshape(owner_count * CAP, local_rows, arrived.shape[3])
    fetched = flattened[owners * CAP + rank_in].reshape(
        req_count, table_width, local_rows, arrived.shape[3]
    )
    prefix_page_list = table_width - STATE_PAGES
    head_count = decay_rates.shape[0]
    mixer_rows = []
    attention_rows = []
    for request in range(req_count):
        request_pages = fetched[request]
        cached_state = request_pages[prefix_page_list:].reshape(
            STATE_PAGES, head_count, HEAD_P // STATE_PAGES, STATE
        )
        cached_state = cached_state.transpose(1, 0, 2, 3).reshape(head_count, HEAD_P, STATE)
        previous_rows = (
            request_pages[:prefix_page_list]
            .reshape(prefix_page_list, kv_local, PAGE, 2 * HEAD_DIM)
            .transpose(1, 0, 2, 3)
        )
        previous_rows = previous_rows.reshape(kv_local, prefix_page_list * PAGE, 2 * HEAD_DIM)
        mixer_rows.append(
            mamba_block(
                ssm_values[request],
                ssm_gate[request],
                ssm_keys[request],
                ssm_queries[request],
                step_sizes[request],
                decay_rates,
                skip_weights,
                norm_gain,
                cached_state,
                new_lengths[request],
            )
        )
        attention_rows.append(
            attend(
                att_queries[request],
                new_keyvals[request],
                previous_rows,
                new_lengths[request],
                cached_lengths[request],
            )
        )
    return (jnp.stack(mixer_rows), jnp.stack(attention_rows))


def solution(mesh):
    return jax.shard_map(
        body,
        mesh=mesh,
        in_specs=(
            P("batch", None, "head"),
            P("batch", None, "head"),
            P("batch", None, "head"),
            P("batch", None, "head"),
            P("batch", None, "head"),
            P("head"),
            P("head"),
            P("head"),
            P("batch", None, "head"),
            P("batch", None, "head"),
            P("batch", "head", None),
            P("batch", None, None),
            P("batch", None),
            P("batch"),
            P("batch"),
        ),
        out_specs=(P("batch", None, "head"), P("batch", None, "head")),
        check_vma=False,
    )
```

profile of v0, /device:TPU:16, one launch (start us, length us, event | category | flops | bytes accessed | tf_op | source)
XLA Modules:
  0.0 383.3 jit_solution(4972829221256878287)
XLA Ops:
  0.7 45.1 %all-gather = s32[32,2,32]{2,1,0:T(2,128)S(1)} all-gather(s32[1,2,32]{2,1,0:T(2,128)} %bitcast.239), channel_id=1, replica_groups=mesh['batch'=32,'head'=8] {'batch'}, dimensions={0}, use_global_device_ids=true | all-gather | bytes 8448 | tf_op jit(solution)/shard_map/all_gather | solution.py:128
  45.9 37.0 %all_gather.6 = s32[64,32,1]{1,2,0:T(1,128)S(1)} all-gather(s32[2,32,1]{1,2,0:T(1,128)} %param.26), channel_id=1, replica_groups=mesh['batch'=32,'head'=8] {'batch'}, dimensions={0}, use_global_device_ids=true | all-gather | bytes 8448 | tf_op jit(solution)/shard_map/all_gather | solution.py:127
  83.7 6.4 %gather_fusion = bf16[128,128,256]{2,1,0:T(8,128)(2,1)} fusion(bf16[32,128,256]{2,1,0:T(8,128)(2,1)S(1)} %copy-done, s32[1024]{0:T(1024)S(1)} %pad_clamp_fusion.1), kind=kCustom, calls=%fused_computation | custom fusion | bytes 16777728 | tf_op jit(solution)/shard_map/gather | solution.py:139
  90.1 7.2 %broadcast_select_fusion = bf16[32,4,128,256]{3,2,1,0:T(8,128)(2,1)} fusion(bf16[32,4,128,256]{3,2,1,0:T(8,128)(2,1)} %bitcast.222, pred[32,4]{1,0:T(8,128)(4,1)S(1)} %copy.103), kind=kLoop, calls=%fused_computation.18 | loop fusion | flops 4194304 | bytes 16777344 | tf_op jit(solution)/shard_map/jit(_where)/select_n | solution.py:140
  97.4 5.3 %all-to-all-start = ((bf16[32,4,128,256]{3,2,1,0:T(8,128)(2,1)}), bf16[32,4,128,256]{3,2,1,0:T(8,128)(2,1)}, u32[]{:S(2)}, u32[]{:S(2)}) async-start(bf16[32,4,128,256]{3,2,1,0:T(8,128)(2,1)} %broadcast_select_fusion), calls=%async_computation | async-start | bytes 16777216 | tf_op jit(solution)/shard_map/all_to_all | solution.py:145
  109.7 1.8 fusion.94
  111.5 1.3 copy.109
  112.8 1.3 copy.116
  114.2 3.4 slice_convert_fusion.1
  117.6 3.0 copy.110
  120.6 1.8 copy.117
  122.9 1.2 iota_compare_fusion.6
  125.8 2.4 pad_add_fusion.1
  128.2 161.9 %all-to-all-done = bf16[32,4,128,256]{3,2,1,0:T(8,128)(2,1)} async-done(((bf16[32,4,128,256]{3,2,1,0:T(8,128)(2,1)}), bf16[32,4,128,256]{3,2,1,0:T(8,128)(2,1)}, u32[]{:S(2)}, u32[]{:S(2)}) %all-to-all-start) | async-done | bytes 8388640 | tf_op jit(solution)/shard_map/all_to_all | solution.py:145
  290.1 6.2 %gather_fusion.1 = bf16[64,128,256]{2,1,0:T(8,128)(2,1)} fusion(bf16[128,128,256]{2,1,0:T(8,128)(2,1)} %bitcast.3, s32[1024]{0:T(1024)S(1)} %pad_clamp_fusion), kind=kCustom, calls=%fused_computation.1 | custom fusion | bytes 8388864 | tf_op jit(solution)/shard_map/gather | solution.py:147
  296.3 4.0 %fusion.93 = (bf16[16,128,256]{2,1,0:T(8,128)(2,1)}, bf16[16,128,256]{2,1,0:T(8,128)(2,1)S(1)}, bf16[16,128,256]{2,1,0:T(8,128)(2,1)}, bf16[16,128,256]{2,1,0:T(8,128)(2,1)}) fusion(bf16[64,128,256]{2,1,0:T(8,128)(2,1)} %gather_fusion.1), kind=kLoop, calls=%fused_computation.142 | loop fusion | bytes 8388608 | tf_op jit(solution)/shard_map/slice | solution.py:161
  300.9 1.5 copy.113
  302.4 1.3 reshape.543
  304.2 6.5 %multiply_reduce_fusion = (f32[256]{0:T(256)S(1)}, f32[256,32,64]{0,2,1:T(8,128)}) fusion(f32[256,32,64]{0,2,1:T(8,128)} %bitcast.232, bf16[256,32,64]{0,2,1:T(8,128)(2,1)} %bitcast.236, f32[32]{0:T(128)S(1)} %copy-done.20, f32[32,256]{1,0:T(8,128)S(1)} %copy-done.14, f32[256,256]{1,0:T(8,128)S(1)} %fusion.60, f32[32,256]{1,0:T(8,128)S(1)} %copy_bitcast_fusion, ...), kind=kOutput, calls=%fused_computation.45 | convolution fusion | flops 287309568 | bytes 7767168 | tf_op jit(solution)/shard_map/hts,shp->thp/dot_general | solution.py:44
  310.7 3.0 copy.118
  314.3 1.5 copy.106
  315.8 1.3 reshape.534
  317.6 6.6 %multiply_reduce_fusion.1 = (f32[256]{0:T(256)S(1)}, f32[256,32,64]{0,2,1:T(8,128)}) fusion(f32[256,32,64]{0,2,1:T(8,128)} %bitcast.231, bf16[256,32,64]{0,2,1:T(8,128)(2,1)} %bitcast.235, f32[32]{0:T(128)S(1)} %copy-done.20, f32[32,256]{1,0:T(8,128)S(1)} %copy-done.13, f32[256,256]{1,0:T(8,128)S(1)} %fusion.65, f32[32,256]{1,0:T(8,128)S(1)} %copy_bitcast_fusion.1, ...), kind=kOutput, calls=%fused_computation.47 | convolution fusion | flops 287309568 | bytes 7767168 | tf_op jit(solution)/shard_map/hts,shp->thp/dot_general | solution.py:44
  324.2 2.9 copy.111
  327.1 10.5 %fusion.2 = (f32[8,256]{1,0:T(8,128)S(1)}, f32[2304,256,8]{1,0,2:T(8,128)}) fusion(pred[256,2304]{0,1:T(8,128)(4,1)S(1)} %get-tuple-element.18, bf16[256,8,128]{0,2,1:T(8,128)(2,1)} %bitcast.230, bf16[1,256,256]{2,1,0:T(8,128)(2,1)S(1)} %get-tuple-element.14, bf16[1,2048,256]{2,1,0:T(8,128)(2,1)} %bitcast.227), kind=kOutput, calls=%fused_computation.10 | convolution fusion | flops 1223292928 | bytes 21176320 | tf_op jit(solution)/shard_map/tkgd,ksd->kgts/dot_general | solution.py:73
  337.6 2.8 fusion.3
  340.5 16.5 %fusion = (f32[8,256]{1,0:T(8,128)S(1)}, f32[8,256]{1,0:T(8,128)S(1)}) fusion(f32[2304,256,8]{1,0,2:T(8,128)} %get-tuple-element.35, f32[8,256]{1,0:T(8,128)S(1)} %get-tuple-element.34, pred[256,2304]{0,1:T(8,128)(4,1)S(1)} %get-tuple-element.18, f32[8,256]{1,0:T(8,128)S(1)} %get-tuple-element.32, f32[2304,256,8]{1,0,2:T(8,128)S(1)} %get-tuple-element.33, ...), kind=kLoop, calls=%fused_computation.8 | loop fusion | flops 37744640 | bytes 38961152 | tf_op jit(solution)/shard_map/reduce_sum | solution.py:88
  357.0 9.8 %fusion.43 = bf16[1,128,8,256]{3,1,2,0:T(8,128)(2,1)S(1)} fusion(f32[8,256]{1,0:T(8,128)S(1)} %get-tuple-element.40, f32[8,256]{1,0:T(8,128)S(1)} %get-tuple-element.34, f32[2304,256,8]{1,0,2:T(8,128)} %get-tuple-element.35, pred[256,2304]{0,1:T(8,128)(4,1)S(1)} %get-tuple-element.18, bf16[1,2048,256]{2,1,0:T(8,128)(2,1)S(1)} %bitcast.228, ...), kind=kOutput, calls=%fused_computation.53 | convolution fusion | flops 1233256448 | bytes 21184768 | tf_op jit(solution)/shard_map/kgts,ksd->tkgd/dot_general | solution.py:89
  367.8 9.8 %fusion.37 = bf16[1,128,8,256]{3,1,2,0:T(8,128)(2,1)S(1)} fusion(f32[8,256]{1,0:T(8,128)S(1)} %get-tuple-element.41, f32[8,256]{1,0:T(8,128)S(1)} %get-tuple-element.32, f32[2304,256,8]{1,0,2:T(8,128)} %copy-done.2, pred[256,2304]{0,1:T(8,128)(4,1)S(1)} %get-tuple-element.19, bf16[1,2048,256]{2,1,0:T(8,128)(2,1)S(1)} %bitcast.226, ...), kind=kOutput, calls=%fused_computation.51 | convolution fusion | flops 1233256448 | bytes 21184768 | tf_op jit(solution)/shard_map/kgts,ksd->tkgd/dot_general | solution.py:89
  377.8 2.9 select_convert_fusion.1
  380.8 1.5 pad_maximum_fusion
  382.3 1.1 pad_maximum_fusion.1
  (100 shorter events, 13.6 us)
Async XLA Ops:
  0.6 83.1 %copy-start = (bf16[32,128,256]{2,1,0:T(8,128)(2,1)S(1)}, bf16[32,128,256]{2,1,0:T(8,128)(2,1)}, u32[]{:S(2)}) copy-start(bf16[32,128,256]{2,1,0:T(8,128)(2,1)} %param.25) | copy-start | bytes 6291460
  97.3 5.8 %copy-start.16 = (s32[2,32,1]{1,2,0:T(1,128)S(1)}, s32[2,32,1]{1,2,0:T(1,128)}, u32[]{:S(2)}) copy-start(s32[2,32,1]{1,2,0:T(1,128)} %param.26) | copy-start | bytes 772
  97.3 6.7 %copy-start.17 = (s32[2]{0:T(128)S(1)}, s32[2]{0:T(128)}, u32[]{:S(2)}) copy-start(s32[2]{0:T(128)} %param.29) | copy-start | bytes 28
  97.3 8.6 %copy-start.11 = (f32[2,256,32]{1,2,0:T(8,128)S(1)}, f32[2,256,32]{1,2,0:T(8,128)}, u32[]{:S(2)}) copy-start(f32[2,256,32]{1,2,0:T(8,128)} %param.19) | copy-start | bytes 196612
  97.4 8.6 %copy-start.19 = (f32[32]{0:T(128)S(1)}, f32[32]{0:T(128)}, u32[]{:S(2)}) copy-start(f32[32]{0:T(128)} %param.20) | copy-start | bytes 388
  97.4 10.3 %copy-start.8 = (bf16[2,256,1024]{2,1,0:T(8,128)(2,1)S(1)}, bf16[2,256,1024]{2,1,0:T(8,128)(2,1)}, u32[]{:S(2)}) copy-start(bf16[2,256,1024]{2,1,0:T(8,128)(2,1)} %param.23) | copy-start | bytes 3145732
  97.4 192.8 %all-to-all-start = ((bf16[32,4,128,256]{3,2,1,0:T(8,128)(2,1)}), bf16[32,4,128,256]{3,2,1,0:T(8,128)(2,1)}, u32[]{:S(2)}, u32[]{:S(2)}) async-start(bf16[32,4,128,256]{3,2,1,0:T(8,128)(2,1)} %broadcast_select_fusion), calls=%async_computation | async-start | bytes 16777216 | tf_op jit(solution)/shard_map/all_to_all | solution.py:145
  117.5 4.8 %copy-start.18 = (s32[2]{0:T(128)S(1)}, s32[2]{0:T(128)}, u32[]{:S(2)}) copy-start(s32[2]{0:T(128)} %param.28) | copy-start | bytes 28
  117.5 7.8 %copy-start.10 = (bf16[2,256,256]{2,1,0:T(8,128)(2,1)S(1)}, bf16[2,256,256]{2,1,0:T(8,128)(2,1)}, u32[]{:S(2)}) copy-start(bf16[2,256,256]{2,1,0:T(8,128)(2,1)} %param.24) | copy-start | bytes 786436
  117.5 7.8 %copy-start.9 = (bf16[2,256,256]{2,1,0:T(8,128)(2,1)S(1)}, bf16[2,256,256]{2,1,0:T(8,128)(2,1)}, u32[]{:S(2)}) copy-start(bf16[2,256,256]{2,1,0:T(8,128)(2,1)} %param.18) | copy-start | bytes 786436
  117.6 7.8 %copy-start.12 = (bf16[2,256,256]{2,1,0:T(8,128)(2,1)S(1)}, bf16[2,256,256]{2,1,0:T(8,128)(2,1)}, u32[]{:S(2)}) copy-start(bf16[2,256,256]{2,1,0:T(8,128)(2,1)} %param.17) | copy-start | bytes 786436
  300.9 3.4 copy-start.14
  300.9 3.4 copy-start.20
  310.7 3.0 copy-start.5
  314.2 3.3 copy-start.13
  327.1 10.6 %copy-start.3 = (bf16[16,128,256]{2,1,0:T(8,128)(2,1)S(1)}, bf16[16,128,256]{2,1,0:T(8,128)(2,1)}, u32[]{:S(2)}) copy-start(bf16[16,128,256]{2,1,0:T(8,128)(2,1)} %get-tuple-element.7) | copy-start | bytes 3145732
  327.1 10.6 %copy-start.6 = (bf16[1,256,1024]{1,2,0:T(8,128)(2,1)S(1)}, bf16[1,256,1024]{1,2,0:T(8,128)(2,1)}, u32[]{:S(2)}) copy-start(bf16[1,256,1024]{1,2,0:T(8,128)(2,1)} %copy.138) | copy-start | bytes 1572868
  340.5 16.5 %copy-start.2 = (f32[2304,256,8]{1,0,2:T(8,128)}, f32[2304,256,8]{1,0,2:T(8,128)S(1)}, u32[]{:S(2)}) copy-start(f32[2304,256,8]{1,0,2:T(8,128)S(1)} %get-tuple-element.33) | copy-start | bytes 56623108
  340.5 16.5 %copy-start.4 = (bf16[16,128,256]{2,1,0:T(8,128)(2,1)S(1)}, bf16[16,128,256]{2,1,0:T(8,128)(2,1)}, u32[]{:S(2)}) copy-start(bf16[16,128,256]{2,1,0:T(8,128)(2,1)} %get-tuple-element.4) | copy-start | bytes 3145732
  367.8 10.0 %copy-start.15 = (f32[2048]{0:T(1024)S(1)}, f32[2048]{0:T(1024)}, u32[]{:S(2)}) copy-start(f32[2048]{0:T(1024)} %param.22) | copy-start | bytes 24580
  377.8 4.5 %copy-start.7 = (bf16[1,256,1024]{2,1,0:T(8,128)(2,1)S(1)}, bf16[1,256,1024]{2,1,0:T(8,128)(2,1)}, u32[]{:S(2)}) copy-start(bf16[1,256,1024]{2,1,0:T(8,128)(2,1)} %copy.127) | copy-start | bytes 1572868
  377.8 5.5 %copy-start.1 = (bf16[32,128,256]{2,1,0:T(8,128)(2,1)S(1)}, bf16[32,128,256]{2,1,0:T(8,128)(2,1)}, u32[]{:S(2)}) copy-start(bf16[32,128,256]{2,1,0:T(8,128)(2,1)} %param.25) | copy-start | bytes 6291460
where the time goes:
time: 384 us; the launch traced here: 383 us
  waiting for transfers between devices  162 us (42%)
  blocking collectives  82.1 us (21%)
  matrix products  47.4 us (12%)
  local copies, waits for them, and re-layouts  45.2 us (12%)
  other arithmetic  40.5 us (11%)
  starting transfers between devices  5.28 us (1%)
    all_to_all x1, waiting for transfers between devices, body(): lax.all_to_all(leaving_rows, 'batch', split_axis=0, concat_axis=0, tiled=...  162 us
    all_gather x1, blocking collectives, body(): lax.all_gather(page_slot, 'batch', axis=0, tiled=True)  45.1 us
    all_gather x1, blocking collectives, body(): lax.all_gather(page_owner, 'batch', axis=0, tiled=True)  37 us
    dot_general x2, matrix products, attend(): jnp.einsum('kgts,ksd->tkgd', probabilities, keyvals[:, :, HEAD_DIM:], pre...  19.6 us
    reduce_sum x1, other arithmetic, attend(): jnp.sum(raised, axis=-1, keepdims=True)  16.5 us
    dot_general x2, matrix products, attend(): jnp.einsum('tkgd,ksd->kgts', grouped_heads, keyvals[:, :, :HEAD_DIM], pre...  13.4 us
    dot_general x2, matrix products, mamba_block(): jnp.einsum('hts,shp->thp', weights, per_head, preferred_element_type=jnp....  13.1 us
  transfers between devices with their start and end apart: 1, of which 1 were waited for; matrix products, arithmetic and copies ran while one was open for 7% of the time, Pallas kernels for 0%

commit v1 on v0

v1 whole, which is shorter than its diff:
```python
import functools

import jax
import jax.numpy as jnp
from jax import lax
from jax.experimental import pallas as pl
from jax.experimental.pallas import tpu as pltpu
from jax.sharding import PartitionSpec as P

HEAD_P = 64
STATE = 256
HEAD_DIM = 128
PAGE = 128
STATE_PAGES = 16
CAP = 4
BLOCK_PAGES = 4
GROUP_HEADS = 4
NEG = float("-inf")
SCORE_SCALE = HEAD_DIM**-0.5 * 1.4426950408889634
LOG2E = 1.4426950408889634
NT = (((1,), (1,)), ((), ()))
VMEM_BYTES = 48 * 1024 * 1024


def fresh_kernel(v_ref, k_ref, q_ref, dsc_ref, dsr_ref, dtr_ref, skip_ref, out_ref, inner_ref):
    new_count = v_ref.shape[1]

    @pl.when(pl.program_id(1) == 0)
    def _():
        inner_ref[...] = lax.dot_general(
            q_ref[0], k_ref[0], NT, preferred_element_type=jnp.float32
        )

    inner = inner_ref[...]
    shape = (new_count, new_count)
    causal = lax.broadcasted_iota(jnp.int32, shape, 0) >= lax.broadcasted_iota(jnp.int32, shape, 1)
    lane = lax.broadcasted_iota(jnp.int32, (new_count, 128), 1)
    for pair in range(GROUP_HEADS // 2):
        cols = slice(pair * 128, pair * 128 + 128)
        pair_values = v_ref[0, :, cols]
        parts = []
        for half in range(2):
            h = pair * 2 + half
            gap = dsr_ref[0, 0, h : h + 1, :] - dsc_ref[0, 0, :, h : h + 1]
            decay = jnp.exp2(jnp.where(causal, gap * LOG2E, NEG))
            weights = (decay * inner * dtr_ref[0, 0, h : h + 1, :]).astype(jnp.bfloat16)
            parts.append(jnp.dot(weights, pair_values, preferred_element_type=jnp.float32))
        fresh = jnp.where(lane < HEAD_P, parts[0], parts[1])
        out_ref[0, :, cols] = fresh + skip_ref[0, :, cols] * pair_values.astype(jnp.float32)


def fresh_part(values, keys, queries, ds_cols, ds_rows, dt_rows, skip_cols):
    req, new_count, width = values.shape
    block = GROUP_HEADS * HEAD_P
    groups = width // block
    return pl.pallas_call(
        fresh_kernel,
        grid=(req, groups),
        out_shape=jax.ShapeDtypeStruct(values.shape, jnp.float32),
        in_specs=[
            pl.BlockSpec((1, new_count, block), lambda r, g: (r, 0, g)),
            pl.BlockSpec((1, new_count, STATE), lambda r, g: (r, 0, 0)),
            pl.BlockSpec((1, new_count, STATE), lambda r, g: (r, 0, 0)),
            pl.BlockSpec((1, 1, new_count, GROUP_HEADS), lambda r, g: (r, g, 0, 0)),
            pl.BlockSpec((1, 1, GROUP_HEADS, new_count), lambda r, g: (r, g, 0, 0)),
            pl.BlockSpec((1, 1, GROUP_HEADS, new_count), lambda r, g: (r, g, 0, 0)),
            pl.BlockSpec((1, 1, block), lambda r, g: (0, 0, g)),
        ],
        out_specs=pl.BlockSpec((1, new_count, block), lambda r, g: (r, 0, g)),
        scratch_shapes=[pltpu.VMEM((new_count, new_count), jnp.float32)],
        compiler_params=pltpu.CompilerParams(
            dimension_semantics=("arbitrary", "arbitrary"), vmem_limit_bytes=VMEM_BYTES
        ),
        cost_estimate=pl.CostEstimate(
            flops=2 * req * 32 * 256 * 256 * 256, bytes_accessed=8 << 20, transcendentals=4 << 20
        ),
        name="ssm_fresh",
    )(values, keys, queries, ds_cols, ds_rows, dt_rows, skip_cols)


def mixer_kernel(
    index_ref, len_ref, fresh_ref, gate_ref, q_ref, dsc_ref, gain_ref, pages_ref, out_ref, states, gated_ref, sems
):
    r = pl.program_id(0)
    req = states.shape[0]
    new_count = q_ref.shape[1]
    groups = dsc_ref.shape[1]

    def copy(n):
        return pltpu.make_async_copy(
            pages_ref.at[index_ref[n]],
            states.at[n // STATE_PAGES, n % STATE_PAGES],
            sems.at[n],
        )

    @pl.when(r == 0)
    def _():
        for n in range(req * STATE_PAGES):
            copy(n).start()

    for k in range(STATE_PAGES):
        copy(r * STATE_PAGES + k).wait()

    block = GROUP_HEADS * HEAD_P
    rows = lax.broadcasted_iota(jnp.int32, (block, block), 0)
    columns = lax.broadcasted_iota(jnp.int32, (block, block), 1)
    source = ((rows >> 2) & 15) * 16 + (rows >> 6) * 4 + (rows & 3)
    perm = (columns == source).astype(jnp.float32).astype(jnp.bfloat16)
    lane = lax.broadcasted_iota(jnp.int32, (new_count, 128), 1)
    queries = q_ref[0]
    square = jnp.zeros((new_count, 128), jnp.float32)
    for g in range(groups):
        rows16 = states[r, :, 16 * g : 16 * g + 16, :].reshape(block, STATE)
        ordered = jnp.dot(perm, rows16, preferred_element_type=jnp.float32).astype(jnp.bfloat16)
        carried = lax.dot_general(queries, ordered, NT, preferred_element_type=jnp.float32)
        fade = jnp.exp(-dsc_ref[0, g])
        for pair in range(GROUP_HEADS // 2):
            cols = slice(g * block + pair * 128, g * block + pair * 128 + 128)
            factor = jnp.where(
                lane < HEAD_P, fade[:, 2 * pair : 2 * pair + 1], fade[:, 2 * pair + 1 : 2 * pair + 2]
            )
            mixed = carried[:, pair * 128 : pair * 128 + 128] * factor + fresh_ref[0, :, cols]
            gate = gate_ref[0, :, cols].astype(jnp.float32)
            gated = mixed * (gate / (1.0 + jnp.exp(-gate)))
            gated_ref[:, cols] = gated
            square = square + gated * gated
    width = gated_ref.shape[1]
    mean_square = jnp.sum(square, axis=1, keepdims=True) * (1.0 / width)
    times = lax.broadcasted_iota(jnp.int32, (new_count, 1), 0)
    scale = lax.rsqrt(mean_square + 1e-05)
    keep = times < len_ref[r]
    for c in range(width // 256):
        cols = slice(c * 256, c * 256 + 256)
        normed = gated_ref[:, cols] * scale * gain_ref[0, :, cols]
        out_ref[0, :, cols] = jnp.where(keep, normed, 0.0).astype(jnp.bfloat16)


def mixer_part(index, lengths, fresh, gate, queries, ds_cols, gain, pages):
    req, new_count, width = fresh.shape
    groups = ds_cols.shape[1]
    return pl.pallas_call(
        mixer_kernel,
        grid_spec=pltpu.PrefetchScalarGridSpec(
            num_scalar_prefetch=2,
            grid=(req,),
            in_specs=[
                pl.BlockSpec((1, new_count, width), lambda r, *_: (r, 0, 0)),
                pl.BlockSpec((1, new_count, width), lambda r, *_: (r, 0, 0)),
                pl.BlockSpec((1, new_count, STATE), lambda r, *_: (r, 0, 0)),
                pl.BlockSpec((1, groups, new_count, GROUP_HEADS), lambda r, *_: (r, 0, 0, 0)),
                pl.BlockSpec((1, 1, width), lambda r, *_: (0, 0, 0)),
                pl.BlockSpec(memory_space=pl.ANY),
            ],
            out_specs=pl.BlockSpec((1, new_count, width), lambda r, *_: (r, 0, 0)),
            scratch_shapes=[
                pltpu.VMEM((req, STATE_PAGES, PAGE, STATE), jnp.bfloat16),
                pltpu.VMEM((new_count, width), jnp.float32),
                pltpu.SemaphoreType.DMA((req * STATE_PAGES,)),
            ],
        ),
        out_shape=jax.ShapeDtypeStruct(fresh.shape, jnp.bfloat16),
        compiler_params=pltpu.CompilerParams(
            dimension_semantics=("arbitrary",), vmem_limit_bytes=VMEM_BYTES
        ),
        cost_estimate=pl.CostEstimate(
            flops=4 * req * 256 * 256 * 2048, bytes_accessed=14 << 20, transcendentals=1 << 20
        ),
        name="ssm_mix",
    )(index, lengths, fresh, gate, queries, ds_cols, gain, pages)


def softmax_step(q, kv, bias, head, acc_ref, top_ref, first):
    scores = lax.dot_general(
        q, kv[:, :HEAD_DIM], NT, preferred_element_type=jnp.float32
    )
    scores = scores * SCORE_SCALE + bias
    width = scores.shape[1] // 128
    best = jnp.max(scores, axis=1, keepdims=True)
    ones = jnp.ones((kv.shape[0], HEAD_DIM), jnp.bfloat16)
    values = jnp.concatenate([kv[:, HEAD_DIM:], ones], axis=1)
    if first:
        top = jnp.broadcast_to(best, (scores.shape[0], 128))
    else:
        old = top_ref[head]
        top = jnp.maximum(old, best)
    raised = jnp.exp2(scores - jnp.concatenate([top] * width, axis=1)).astype(jnp.bfloat16)
    summed = jnp.dot(raised, values, preferred_element_type=jnp.float32)
    if not first:
        shrink = jnp.exp2(old - top)
        summed = summed + acc_ref[head] * jnp.concatenate([shrink, shrink], axis=1)
    acc_ref[head] = summed
    top_ref[head] = top


def new_kernel(q_ref, kv_ref, acc_out, top_out):
    heads = q_ref.shape[2] // HEAD_DIM
    count = q_ref.shape[1]
    shape = (count, count)
    causal = lax.broadcasted_iota(jnp.int32, shape, 0) >= lax.broadcasted_iota(jnp.int32, shape, 1)
    bias = jnp.where(causal, 0.0, NEG)
    kv = kv_ref[0]
    for head in range(heads):
        q = q_ref[0, :, head * HEAD_DIM : (head + 1) * HEAD_DIM]
        softmax_step(q, kv, bias, head, acc_out.at[0], top_out.at[0], True)


def attend_new(queries, new_kv):
    req, count, width = queries.shape
    heads = width // HEAD_DIM
    return pl.pallas_call(
        new_kernel,
        grid=(req,),
        out_shape=(
            jax.ShapeDtypeStruct((req, heads, count, 2 * HEAD_DIM), jnp.float32),
            jax.ShapeDtypeStruct((req, heads, count, HEAD_DIM), jnp.float32),
        ),
        in_specs=[
            pl.BlockSpec((1, count, width), lambda r: (r, 0, 0)),
            pl.BlockSpec((1, count, 2 * HEAD_DIM), lambda r: (r, 0, 0)),
        ],
        out_specs=(
            pl.BlockSpec((1, heads, count, 2 * HEAD_DIM), lambda r: (r, 0, 0, 0)),
            pl.BlockSpec((1, heads, count, HEAD_DIM), lambda r: (r, 0, 0, 0)),
        ),
        compiler_params=pltpu.CompilerParams(
            dimension_semantics=("arbitrary",), vmem_limit_bytes=VMEM_BYTES
        ),
        cost_estimate=pl.CostEstimate(
            flops=8 * req * 2048 * 256 * 128, bytes_accessed=8 << 20, transcendentals=1 << 20
        ),
        name="attend_new",
    )(queries, new_kv)


def paged_kernel(last, index_ref, seen_ref, blocks_ref, len_ref, q_ref, acc_in, top_in, pages_ref, *rest):
    if last:
        out_ref, kv_buf, acc_ref, top_ref, sems = rest
    else:
        acc_out, top_out, kv_buf, sems = rest
        acc_ref, top_ref = acc_out.at[0], top_out.at[0]
    r = pl.program_id(0)
    heads = q_ref.shape[2] // HEAD_DIM
    count = q_ref.shape[1]
    per_request = index_ref.shape[0] // len_ref.shape[0]
    base = r * per_request
    blocks = blocks_ref[r]

    def copy(block, slot, i):
        return pltpu.make_async_copy(
            pages_ref.at[index_ref[base + block * BLOCK_PAGES + i]],
            kv_buf.at[slot, pl.ds(i * PAGE, PAGE)],
            sems.at[slot, i],
        )

    @pl.when(blocks > 0)
    def _():
        for i in range(BLOCK_PAGES):
            copy(0, 0, i).start()

    acc_ref[...] = acc_in[0]
    top_ref[...] = top_in[0]
    lane = lax.broadcasted_iota(jnp.int32, (1, PAGE), 1)

    def step(block, carry):
        slot = lax.rem(block, 2)

        @pl.when(block + 1 < blocks)
        def _():
            for i in range(BLOCK_PAGES):
                copy(block + 1, 1 - slot, i).start()

        for i in range(BLOCK_PAGES):
            copy(block, slot, i).wait()
        bias = jnp.concatenate(
            [
                jnp.where(lane < seen_ref[base + block * BLOCK_PAGES + i], 0.0, NEG)
                for i in range(BLOCK_PAGES)
            ],
            axis=1,
        )
        kv = kv_buf[slot]
        for head in range(heads):
            q = q_ref[0, :, head * HEAD_DIM : (head + 1) * HEAD_DIM]
            softmax_step(q, kv, bias, head, acc_ref, top_ref, False)
        return carry

    lax.fori_loop(0, blocks, step, 0)
    if last:
        keep = lax.broadcasted_iota(jnp.int32, (count, 1), 0) < len_ref[r]
        for head in range(heads):
            acc = acc_ref[head]
            result = acc[:, :HEAD_DIM] / acc[:, HEAD_DIM:]
            out_ref[0, :, head * HEAD_DIM : (head + 1) * HEAD_DIM] = jnp.where(
                keep, result, 0.0
            ).astype(jnp.bfloat16)


def attend_paged(last, index, seen, blocks, lengths, queries, acc, top, pages):
    req, count, width = queries.shape
    heads = width // HEAD_DIM
    acc_spec = pl.BlockSpec((1, heads, count, 2 * HEAD_DIM), lambda r, *_: (r, 0, 0, 0))
    top_spec = pl.BlockSpec((1, heads, count, HEAD_DIM), lambda r, *_: (r, 0, 0, 0))
    q_spec = pl.BlockSpec((1, count, width), lambda r, *_: (r, 0, 0))
    scratch = [pltpu.VMEM((2, BLOCK_PAGES * PAGE, 2 * HEAD_DIM), jnp.bfloat16)]
    if last:
        out_shape = jax.ShapeDtypeStruct(queries.shape, jnp.bfloat16)
        out_specs = q_spec
        scratch += [
            pltpu.VMEM((heads, count, 2 * HEAD_DIM), jnp.float32),
            pltpu.VMEM((heads, count, HEAD_DIM), jnp.float32),
        ]
    else:
        out_shape = (
            jax.ShapeDtypeStruct(acc.shape, jnp.float32),
            jax.ShapeDtypeStruct(top.shape, jnp.float32),
        )
        out_specs = (acc_spec, top_spec)
    return pl.pallas_call(
        functools.partial(paged_kernel, last),
        grid_spec=pltpu.PrefetchScalarGridSpec(
            num_scalar_prefetch=4,
            grid=(req,),
            in_specs=[q_spec, acc_spec, top_spec, pl.BlockSpec(memory_space=pl.ANY)],
            out_specs=out_specs,
            scratch_shapes=scratch + [pltpu.SemaphoreType.DMA((2, BLOCK_PAGES))],
        ),
        out_shape=out_shape,
        compiler_params=pltpu.CompilerParams(
            dimension_semantics=("arbitrary",), vmem_limit_bytes=VMEM_BYTES
        ),
        cost_estimate=pl.CostEstimate(
            flops=8 * req * 2048 * 1024 * 128, bytes_accessed=16 << 20, transcendentals=4 << 20
        ),
        name="attend_paged",
    )(index, seen, blocks, lengths, queries, acc, top, pages)


def page_lists(chosen, rows, seen):
    req, count = chosen.shape
    flags = chosen.astype(jnp.int32)
    place = jnp.cumsum(flags, axis=1) - flags
    hit = chosen[:, :, None] & (place[:, :, None] == jnp.arange(count, dtype=jnp.int32)[None, None, :])
    listed = jnp.sum(jnp.where(hit, rows[:, :, None], 0), axis=1)
    limits = jnp.sum(jnp.where(hit, seen[:, :, None], 0), axis=1)
    total = jnp.sum(flags, axis=1)
    valid = jnp.arange(count, dtype=jnp.int32)[None, :] < total[:, None]
    listed = jnp.where(valid, listed, listed[:, :1])
    blocks = (total + BLOCK_PAGES - 1) // BLOCK_PAGES
    return listed.reshape(-1), limits.reshape(-1), blocks


def body(
    ssm_values,
    ssm_gate,
    ssm_keys,
    ssm_queries,
    step_sizes,
    decay_rates,
    skip_weights,
    norm_gain,
    att_queries,
    new_keyvals,
    page_pool,
    page_owner,
    page_slot,
    new_lengths,
    cached_lengths,
):
    owner_count = lax.axis_size("batch")
    my_index = lax.axis_index("batch")
    req_count, new_count, width = ssm_values.shape
    head_count = decay_rates.shape[0]
    groups = head_count // GROUP_HEADS
    pool_dev = page_pool.shape[0]
    table_width = page_owner.shape[1]
    prefix_pages = table_width - STATE_PAGES
    block_rows = req_count * table_width

    owners = page_owner.reshape(block_rows)
    codes = owners * pool_dev + page_slot.reshape(block_rows)
    all_codes = lax.all_to_all(
        jnp.broadcast_to(codes[None], (owner_count, block_rows)), "batch", 0, 0, tiled=True
    )

    capacity = jnp.arange(CAP, dtype=jnp.int32)
    owned = (all_codes // pool_dev == my_index).astype(jnp.int32)
    ahead = jnp.cumsum(owned, axis=1) - owned
    picked = (owned[:, :, None] == 1) & (ahead[:, :, None] == capacity[None, None, :])
    slots = jnp.sum(jnp.where(picked, (all_codes % pool_dev)[:, :, None] + 1, 0), axis=1) - 1
    leaving = page_pool[jnp.maximum(slots.reshape(-1), 0)]
    arrived = lax.all_to_all(
        leaving.reshape((owner_count, CAP) + page_pool.shape[1:]), "batch", 0, 0, tiled=True
    )

    decay_sum = jnp.cumsum(step_sizes * decay_rates[None, None, :], axis=1)
    ds_cols = decay_sum.reshape(req_count, new_count, groups, GROUP_HEADS).transpose(0, 2, 1, 3)
    ds_rows = ds_cols.transpose(0, 1, 3, 2)
    dt_rows = step_sizes.reshape(req_count, new_count, groups, GROUP_HEADS).transpose(0, 2, 3, 1)
    skip_cols = jnp.repeat(skip_weights, HEAD_P).reshape(1, 1, width)
    fresh = fresh_part(ssm_values, ssm_keys, ssm_queries, ds_cols, ds_rows, dt_rows, skip_cols)
    acc, top = attend_new(att_queries, new_keyvals)

    order = jnp.arange(block_rows, dtype=jnp.int32)
    earlier = (owners[:, None] == owners[None, :]) & (order[None, :] < order[:, None])
    rank = jnp.sum(earlier.astype(jnp.int32), axis=1)
    landed = (owners * CAP + rank).reshape(req_count, table_width)
    seen = jnp.clip(
        cached_lengths[:, None] - jnp.arange(prefix_pages, dtype=jnp.int32)[None, :] * PAGE, 0, PAGE
    )
    listed, limits, blocks = page_lists(seen > 0, landed[:, :prefix_pages], seen)

    pages = arrived.reshape((owner_count * CAP,) + page_pool.shape[1:])
    attention = attend_paged(
        True, listed, limits, blocks, new_lengths, att_queries, acc, top, pages
    )
    mixer = mixer_part(
        landed[:, prefix_pages:].reshape(-1),
        new_lengths,
        fresh,
        ssm_gate,
        ssm_queries,
        ds_cols,
        norm_gain.reshape(1, 1, width),
        pages,
    )
    return mixer, attention


def solution(mesh):
    return jax.shard_map(
        body,
        mesh=mesh,
        in_specs=(
            P("batch", None, "head"),
            P("batch", None, "head"),
            P("batch", None, "head"),
            P("batch", None, "head"),
            P("batch", None, "head"),
            P("head"),
            P("head"),
            P("head"),
            P("batch", None, "head"),
            P("batch", None, "head"),
            P("batch", "head", None),
            P("batch", None, None),
            P("batch", None),
            P("batch"),
            P("batch"),
        ),
        out_specs=(P("batch", None, "head"), P("batch", None, "head")),
        check_vma=False,
    )
```

time: 384 us -> 256 us (0.67)
  blocking collectives: 82.1 us -> 0 us
  matrix products: 47.4 us -> 0 us
  Pallas kernels: 0 us -> 37.6 us
  other arithmetic: 40.5 us -> 8.97 us
  local copies, waits for them, and re-layouts: 45.2 us -> 27.2 us
  starting transfers between devices: 5.28 us -> 16.4 us
    all_gather x2 -> x0, blocking collectives: 82.1 us -> none  [the longest x1 45.1 us: body(): lax.all_gather(page_slot, 'batch', axis=0, tiled=True)]
    dot_general x10 -> x0, matrix products: 47.4 us -> none  [the longest x2 19.6 us: attend(): jnp.einsum('kgts,ksd->tkgd', probabilities, keyvals[:, :, HEAD_DIM:], pre...]
    pallas_call x0 -> x4, Pallas kernels: none -> 37.6 us  [the longest x1 15.7 us: attend_paged(): pl.pallas_call(functools.partial(paged_kernel, last), grid_spec=pltpu.Pre...]
    reduce_sum x3 -> x4, other arithmetic: 16.8 us -> 2.42 us  [the longest x1 1.45 us: body(): rank = jnp.sum(earlier.astype(jnp.int32), axis=1)]
    all_to_all x1 -> x2, starting transfers between devices: 5.28 us -> 16.4 us  [the longest x1 11.3 us: body(): lax.all_to_all(jnp.broadcast_to(codes[None], (owner_count, block_rows)),...]
    slice x11 -> x2, local copies, waits for them, and re-layouts: 10.9 us -> 0.29 us  [the longest x3 4.41 us: body(): ssm_values[request]]
    unnamed x45 -> x43, local copies, waits for them, and re-layouts: 2.64 us -> 9.95 us
    select_n x2, other arithmetic: 7.23 us -> 0.72 us  [the longest x1 0.71 us: page_lists(): listed = jnp.where(valid, listed, listed[:, :1])]
  transfers between devices with their start and end apart: 1 -> 2, of which waited for: 1 -> 2; matrix products, arithmetic and copies ran while one was open for 7% -> 6% of each run, Pallas kernels for 0% -> 5%
where the time goes in v1:
time: 256 us; the launch traced here: 254 us
  waiting for transfers between devices  163 us (64%)
  Pallas kernels  37.6 us (15%)
  local copies, waits for them, and re-layouts  27.2 us (11%)
  starting transfers between devices  16.4 us (6%)
  other arithmetic  8.97 us (4%)
    all_to_all x1, waiting for transfers between devices, body(): lax.all_to_all(leaving.reshape((owner_count, CAP) + page_pool.shape[1:]),...  153 us
    pallas_call x1, Pallas kernels, attend_paged(): pl.pallas_call(functools.partial(paged_kernel, last), grid_spec=pltpu.Pre...  15.7 us
    all_to_all x1, starting transfers between devices, body(): lax.all_to_all(jnp.broadcast_to(codes[None], (owner_count, block_rows)),...  11.3 us
    pallas_call x1, Pallas kernels, fresh_part(): pl.pallas_call(fresh_kernel, grid=(req, groups), out_shape=jax.ShapeDtype...  10.5 us
    unnamed x43, local copies, waits for them, and re-layouts  9.95 us
    all_to_all x1, waiting for transfers between devices, body(): lax.all_to_all(jnp.broadcast_to(codes[None], (owner_count, block_rows)),...  9.82 us
    pallas_call x1, Pallas kernels, mixer_part(): pl.pallas_call(mixer_kernel, grid_spec=pltpu.PrefetchScalarGridSpec(num_s...  8.34 us
    gather x1, local copies, waits for them, and re-layouts, body(): leaving = page_pool[jnp.maximum(slots.reshape(-1), 0)]  6.39 us
  transfers between devices with their start and end apart: 2, of which 2 were waited for; matrix products, arithmetic and copies ran while one was open for 6% of the time, Pallas kernels for 5%

profile of v1, /device:TPU:16, one launch (start us, length us, event | category | flops | bytes accessed | tf_op | source)
XLA Modules:
  0.0 253.7 jit_solution(16568637201391150064)
XLA Ops:
  1.2 1.5 fusion.10
  2.7 0.8 reshape.314
  4.1 11.3 %all-to-all-start = ((s32[32,1,64]{2,1,0:T(1,128)}), s32[32,1,64]{2,1,0:T(1,128)S(1)}, u32[]{:S(2)}, u32[]{:S(2)}) async-start(s32[32,1,64]{2,1,0:T(1,128)} %broadcast_in_dim.67), calls=%async_computation | async-start | bytes 32768 | tf_op jit(solution)/shard_map/all_to_all | solution.py:381
  15.4 9.8 %all-to-all-done = s32[32,1,64]{2,1,0:T(1,128)S(1)} async-done(((s32[32,1,64]{2,1,0:T(1,128)}), s32[32,1,64]{2,1,0:T(1,128)S(1)}, u32[]{:S(2)}, u32[]{:S(2)}) %all-to-all-start) | async-done | bytes 8224 | tf_op jit(solution)/shard_map/all_to_all | solution.py:381
  25.9 6.4 %gather_fusion = bf16[128,128,256]{2,1,0:T(8,128)(2,1)} fusion(bf16[32,128,256]{2,1,0:T(8,128)(2,1)S(1)} %copy-done, s32[1024]{0:T(1024)S(1)} %pad_clamp_fusion), kind=kCustom, calls=%fused_computation | custom fusion | bytes 16777728 | tf_op jit(solution)/shard_map/gather | solution.py:390
  32.3 5.1 %all-to-all-start.1 = ((bf16[32,4,128,256]{3,2,1,0:T(8,128)(2,1)}), bf16[32,4,128,256]{3,2,1,0:T(8,128)(2,1)}, u32[]{:S(2)}, u32[]{:S(2)}) async-start(bf16[32,4,128,256]{3,2,1,0:T(8,128)(2,1)} %bitcast.32), calls=%async_computation.1 | async-start | bytes 16777216 | tf_op jit(solution)/shard_map/all_to_all | solution.py:391
  37.5 1.1 reduce-window.6
  39.1 2.0 copy.32
  41.0 0.9 reshape.312
  41.9 0.7 convert_reduce_fusion.1
  43.2 0.9 reduce_window_sum.40
  44.1 1.4 convert_reduce_fusion
  45.5 1.3 reduce_sum.48
  46.9 0.7 add.58
  48.4 0.7 compare_select_fusion
  49.7 0.7 reshape.317.seen_ref
  50.3 1.3 reshape.308.index_ref
  51.6 1.3 broadcast_in_dim.66
  53.0 0.8 reshape_reshape.3.skip_ref
  53.8 0.9 copy-done.15
  54.7 3.1 %attend_new.1 = (f32[2,8,256,256]{3,2,1,0:T(8,128)}, f32[2,8,256,128]{3,2,1,0:T(8,128)S(1)}) custom-call(bf16[2,256,1024]{2,1,0:T(8,128)(2,1)S(1)} %copy-done.8, bf16[2,256,256]{2,1,0:T(8,128)(2,1)S(1)} %copy-done.15), custom_call_target="tpu_custom_call" | custom-call | flops 1073741824 | bytes 8388608 | tf_op jit(solution)/shard_map/attend_new/pallas_call | solution.py:210
  57.8 1.4 copy-done.5
  59.2 1.6 copy-done.3
  60.8 0.9 copy-done.9
  61.8 10.5 %ssm_fresh.1.fresh_ref = f32[2,256,2048]{2,1,0:T(8,128)} custom-call(bf16[2,256,2048]{2,1,0:T(8,128)(2,1)S(1)} %copy-done.3, bf16[2,256,256]{2,1,0:T(8,128)(2,1)S(1)} %copy-done.9, bf16[2,256,256]{2,1,0:T(8,128)(2,1)S(1)} %copy-done.7, f32[2,8,256,4]{3,2,1,0:T(8,128)S(1)} %bitcast.27, f32[2,8,4,256]{3,2,1,0:T(4,128)S(1)} %bitcast.29, ...), custom_call_target="tpu_custom_call" | custom-call | flops 2147483648 | bytes 8388608 | tf_op jit(solution)/shard_map/ssm_fresh/pallas_call | solution.py:56
  72.3 152.8 %all-to-all-done.1 = bf16[32,4,128,256]{3,2,1,0:T(8,128)(2,1)} async-done(((bf16[32,4,128,256]{3,2,1,0:T(8,128)(2,1)}), bf16[32,4,128,256]{3,2,1,0:T(8,128)(2,1)}, u32[]{:S(2)}, u32[]{:S(2)}) %all-to-all-start.1) | async-done | bytes 8388640 | tf_op jit(solution)/shard_map/all_to_all | solution.py:391
  225.1 1.6 copy-done.2
  226.7 1.6 copy-done.4
  228.3 0.7 copy-done.11
  228.9 0.7 copy-done.14
  229.6 8.3 %ssm_mix.1 = bf16[2,256,2048]{2,1,0:T(8,128)(2,1)} custom-call(s32[32]{0:T(128)S(1)} %copy-done.14, s32[2]{0:T(128)S(1)} %copy-done.11, f32[2,256,2048]{2,1,0:T(8,128)} %ssm_fresh.1.fresh_ref, bf16[2,256,2048]{2,1,0:T(8,128)(2,1)S(1)} %copy-done.4, bf16[2,256,256]{2,1,0:T(8,128)(2,1)S(1)} %copy-done.7, f32[2,8,256,4]{3,2,1,0:T(8,128)S(1)} %bitcast.28, ...), custom_call_target="tpu_custom_call" | custom-call | flops 1073741824 | bytes 14680064 | tf_op jit(solution)/shard_map/ssm_mix/pallas_call | solution.py:141
  238.0 15.7 %attend_paged.1 = bf16[2,256,1024]{2,1,0:T(8,128)(2,1)} custom-call(s32[32]{0:T(128)S(1)} %copy-done.12, s32[32]{0:T(128)S(1)} %copy-done.13, s32[2]{0:T(128)S(1)} %and_select_fusion.blocks_ref, s32[2]{0:T(128)S(1)} %copy-done.11, bf16[2,256,1024]{2,1,0:T(8,128)(2,1)S(1)} %copy-done.8, f32[2,8,256,256]{3,2,1,0:T(8,128)} %get-tuple-element.4.acc_in, ...), custom_call_target="tpu_custom_call" | custom-call | flops 4294967296 | bytes 16777216 | tf_op jit(solution)/shard_map/attend_paged/pallas_call | solution.py:318
  (61 shorter events, 4.3 us)
Async XLA Ops:
  0.6 25.3 %copy-start = (bf16[32,128,256]{2,1,0:T(8,128)(2,1)S(1)}, bf16[32,128,256]{2,1,0:T(8,128)(2,1)}, u32[]{:S(2)}) copy-start(bf16[32,128,256]{2,1,0:T(8,128)(2,1)} %param.25) | copy-start | bytes 6291460
  2.7 29.6 %copy-start.20 = (s32[64]{0:T(128)}, s32[64]{0:T(128)S(1)}, u32[]{:S(2)}) copy-start(s32[64]{0:T(128)S(1)} %eq.68) | copy-start | bytes 772
  4.1 21.2 %all-to-all-start = ((s32[32,1,64]{2,1,0:T(1,128)}), s32[32,1,64]{2,1,0:T(1,128)S(1)}, u32[]{:S(2)}, u32[]{:S(2)}) async-start(s32[32,1,64]{2,1,0:T(1,128)} %broadcast_in_dim.67), calls=%async_computation | async-start | bytes 32768 | tf_op jit(solution)/shard_map/all_to_all | solution.py:381
  32.3 5.1 %copy-start.16 = (f32[2,256,32]{1,2,0:T(8,128)S(1)}, f32[2,256,32]{1,2,0:T(8,128)}, u32[]{:S(2)}) copy-start(f32[2,256,32]{1,2,0:T(8,128)} %param.19) | copy-start | bytes 196612
  32.3 5.1 %copy-start.18 = (f32[32]{0:T(128)S(1)}, f32[32]{0:T(128)}, u32[]{:S(2)}) copy-start(f32[32]{0:T(128)} %param.20) | copy-start | bytes 388
  32.3 9.6 %copy-start.19 = (s32[2]{0:T(128)S(1)}, s32[2]{0:T(128)}, u32[]{:S(2)}) copy-start(s32[2]{0:T(128)} %param.29) | copy-start | bytes 28
  32.3 21.5 %copy-start.8 = (bf16[2,256,1024]{2,1,0:T(8,128)(2,1)S(1)}, bf16[2,256,1024]{2,1,0:T(8,128)(2,1)}, u32[]{:S(2)}) copy-start(bf16[2,256,1024]{2,1,0:T(8,128)(2,1)} %q_ref.7) | copy-start | bytes 3145732
  32.3 192.8 %all-to-all-start.1 = ((bf16[32,4,128,256]{3,2,1,0:T(8,128)(2,1)}), bf16[32,4,128,256]{3,2,1,0:T(8,128)(2,1)}, u32[]{:S(2)}, u32[]{:S(2)}) async-start(bf16[32,4,128,256]{3,2,1,0:T(8,128)(2,1)} %bitcast.32), calls=%async_computation.1 | async-start | bytes 16777216 | tf_op jit(solution)/shard_map/all_to_all | solution.py:391
  37.4 21.8 %copy-start.7 = (bf16[2,256,256]{2,1,0:T(8,128)(2,1)S(1)}, bf16[2,256,256]{2,1,0:T(8,128)(2,1)}, u32[]{:S(2)}) copy-start(bf16[2,256,256]{2,1,0:T(8,128)(2,1)} %q_ref.5) | copy-start | bytes 786436
  53.8 1.0 copy-start.15
  54.7 4.5 %copy-start.1 = (f32[2,256,8,4]{3,1,2,0:T(8,128)S(1)}, f32[2,256,8,4]{3,1,2,0:T(8,128)}, u32[]{:S(2)}) copy-start(f32[2,256,8,4]{3,1,2,0:T(8,128)} %copy.32) | copy-start | bytes 196612
  57.8 1.4 copy-start.5
  59.2 1.6 copy-start.3
  60.8 0.9 copy-start.9
  61.8 10.5 %copy-start.17 = (s32[2]{0:T(128)S(1)}, s32[2]{0:T(128)}, u32[]{:S(2)}) copy-start(s32[2]{0:T(128)} %get-tuple-element.8) | copy-start | bytes 28
  61.8 163.3 %copy-start.10 = (f32[2048]{0:T(1024)S(1)}, f32[2048]{0:T(1024)}, u32[]{:S(2)}) copy-start(f32[2048]{0:T(1024)} %param.22) | copy-start | bytes 24580
  225.1 1.6 copy-start.2
  226.7 1.6 copy-start.4
  228.3 0.7 copy-start.11
  228.9 0.7 copy-start.14
  229.6 8.4 %copy-start.6 = (f32[2,8,256,128]{3,2,1,0:T(8,128)S(1)}, f32[2,8,256,128]{3,2,1,0:T(8,128)}, u32[]{:S(2)}) copy-start(f32[2,8,256,128]{3,2,1,0:T(8,128)} %copy-done.5) | copy-start | bytes 6291460
  229.6 8.4 %copy-start.12 = (s32[32]{0:T(128)S(1)}, s32[32]{0:T(128)}, u32[]{:S(2)}) copy-start(s32[32]{0:T(128)} %select_n.57.index_ref) | copy-start | bytes 388
  229.6 8.4 %copy-start.13 = (s32[32]{0:T(128)S(1)}, s32[32]{0:T(128)}, u32[]{:S(2)}) copy-start(s32[32]{0:T(128)} %reshape.317.seen_ref) | copy-start | bytes 388
